TPU v7x, 256 devices: a whole 4x4x8 slice. The times are simulated.
256 devices in a mesh: dp: 8 (over z), cls: 32 (over y, x, core).
Axes of the slice: x: 4, y: 4, z: 8, core: 2. Of those that a mesh axis runs over, the one named last changes fastest.
Arguments:
- weak_embed: bfloat16 [512, 512], P('dp'), may hold values from -6 to 6
- strong_embed: bfloat16 [512, 512], P('dp'), may hold values from -0.0625 to 0.0625
- centers: bfloat16 [1048576, 512], P(('dp', 'cls')), may hold values from -0.0625 to 0.0625
- marginal: float32 [1048576], P(('dp', 'cls')), may hold values from 0.25 to 45
- pseudo_label: int32 [512], P('dp'), may hold values from 0 to 1048575
- confident: int32 [512], P('dp'), may hold values 0 or 1
Outputs:
- new_marginal: float32 [1048576], P(('dp', 'cls'))
- center_grad: bfloat16 [1048576, 512], P(('dp', 'cls'))
- embed_grad: float32 [512, 512], P('dp')
- loss: float32 [], replicated
All inputs are finite; a program needn't handle non-finite values. No bound on the sum of `confident` on one device may be relied on, other than what follows from the above.
Results may differ from a plain program's by a relative error of at most 0.00155.
The roundings to bfloat16 on the way count: a program that leaves them out, or rounds other values in their place, can miss the bound.
Values may be sent and summed in bfloat16 or wider, within the bound.
A program may use at most 128 MiB of HBM per device.

v0:
```python
import jax
import jax.numpy as jnp
from jax import lax
from jax.sharding import PartitionSpec as P

SCALE = 64.0
MARGIN = 0.35
MOMENTUM = 0.9
EPS = 1e-06


def unit_rows(values):
    exact = values.astype(jnp.float32)
    inverse = lax.rsqrt(jnp.sum(exact * exact, axis=-1, keepdims=True) + EPS)
    return (exact * inverse, inverse)


def body(weak_embed, strong_embed, centers, marginal, pseudo_label, confident):
    img = strong_embed.shape[0]
    cls_dev = centers.shape[0]
    weak_exact, _ = unit_rows(weak_embed)
    strong_exact, strong_inv = unit_rows(strong_embed)
    stacked = jnp.stack([weak_exact.astype(jnp.bfloat16), strong_exact.astype(jnp.bfloat16)])
    views, labels, flag_ints = (
        lax.all_gather(stacked, "dp", axis=1, tiled=True),
        lax.all_gather(pseudo_label, "dp", axis=0, tiled=True),
        lax.all_gather(confident, "dp", axis=0, tiled=True),
    )
    row_count = views.shape[1]
    width = views.shape[2]
    flags = flag_ints.astype(jnp.float32)
    center_exact, center_inv = unit_rows(centers)
    center_unit = center_exact.astype(jnp.bfloat16)
    scores = lax.dot_general(
        views.reshape(2 * row_count, width),
        center_unit,
        (((1,), (1,)), ((), ())),
        preferred_element_type=jnp.float32,
    )
    teach = jnp.exp(SCALE * (scores[:row_count] - 1.0))
    offset = (lax.axis_index("dp") * lax.axis_size("cls") + lax.axis_index("cls")) * cls_dev
    ids = offset + jnp.arange(cls_dev, dtype=jnp.int32)
    hit = (labels[:, None] == ids[None, :]).astype(jnp.float32)
    stud = SCALE * (scores[row_count:] - MARGIN * hit)
    teach_part = jnp.sum(teach, axis=1)
    stud_part = jnp.sum(jnp.exp(stud - SCALE), axis=1)
    label_part = jnp.sum(hit * stud, axis=1)
    classes_total = cls_dev * lax.axis_size("dp") * lax.axis_size("cls")
    teacher_total = lax.psum(teach_part, ("dp", "cls"))
    share = teach / teacher_total[:, None]
    batch = classes_total / row_count * jnp.sum(share, axis=0)
    fresh = MOMENTUM * marginal + (1.0 - MOMENTUM) * batch
    raw = share / fresh[None, :]
    fresh, raw, q_part, r_part = (fresh, raw, jnp.sum(raw, axis=1), jnp.sum(raw * stud, axis=1))
    aligned_total, aligned_cross = lax.psum((q_part, r_part), ("dp", "cls"))
    student_total, label_logit = lax.psum((stud_part, label_part), ("dp", "cls"))
    loss = (
        jnp.sum(
            flags
            * (
                SCALE
                + jnp.log(student_total)
                - 0.5 * label_logit
                - 0.5 * aligned_cross / aligned_total
            )
        )
        / img
    )
    grad = (
        SCALE
        / img
        * flags[:, None]
        * (
            jnp.exp(stud - SCALE) / student_total[:, None]
            - 0.5 * hit
            - 0.5 * raw / aligned_total[:, None]
        )
    )
    grad = grad.astype(jnp.bfloat16)
    unit_part = jnp.dot(grad, center_unit, preferred_element_type=jnp.float32)
    unit_total = lax.psum(unit_part, ("dp", "cls"))
    unit_grad = lax.dynamic_slice_in_dim(unit_total, lax.axis_index("dp") * img, img, 0)
    embed_grad = (
        unit_grad - strong_exact * jnp.sum(strong_exact * unit_grad, axis=1, keepdims=True)
    ) * strong_inv
    cgrad = lax.dot_general(
        grad, views[1], (((0,), (0,)), ((), ())), preferred_element_type=jnp.float32
    )
    cgrad = (
        cgrad - center_exact * jnp.sum(center_exact * cgrad, axis=1, keepdims=True)
    ) * center_inv
    return (fresh, cgrad.astype(jnp.bfloat16), embed_grad, loss)


def solution(mesh):
    placed = (
        P("dp", None),
        P("dp", None),
        P(("dp", "cls"), None),
        P(("dp", "cls")),
        P("dp"),
        P("dp"),
    )
    return jax.shard_map(
        body,
        mesh=mesh,
        in_specs=placed,
        out_specs=(P(("dp", "cls")), P(("dp", "cls"), None), P("dp", None), P()),
        check_vma=False,
    )
```

profile of v0, /device:TPU:2, one launch (start us, length us, event | category | flops | bytes accessed | tf_op | source)
XLA Modules:
  0.0 508.1 jit_solution(5591353796502979499)
XLA Ops:
  7.2 1.0 fusion.32
  8.2 1.0 fusion.27
  9.2 1.0 fusion.33
  10.2 0.7 pad_maximum_fusion
  10.9 6.3 %copy.10 = bf16[4096,512]{0,1:T(8,128)(2,1)} copy(bf16[4096,512]{1,0:T(8,128)(2,1)} %param.8) | data formatting | bytes 8388608 | tf_op args[2]
  19.0 16.2 %all-reduce.2 = (s32[512]{0:T(512)S(1)}, s32[512]{0:T(512)S(1)}) all-reduce(s32[512]{0:T(512)S(1)} %dynamic-update-slice.1, s32[512]{0:T(512)S(1)} %dynamic-update-slice), channel_id=1, replica_groups=mesh['dp'=8,'cls'=32] {'dp'}, use_global_device_ids=true, to_apply=%add.1 | all-reduce | flops 1024 | bytes 8192
  35.2 3.1 fusion.7
  38.3 14.4 %all-gather.2.cloned.1.call-done = bf16[2,512,512]{2,1,0:T(8,128)(2,1)} async-done(((bf16[2,64,512]{2,1,0:T(8,128)(2,1)}), bf16[2,512,512]{2,1,0:T(8,128)(2,1)}) %all-gather.2.cloned.1.call-update) | async-done | bytes 1048592 | tf_op jit(solution)/shard_map/all_gather | solution.py:25
  52.7 6.6 %fusion.21 = f32[1024,4096]{1,0:T(8,128)S(1)} fusion(bf16[1024,512]{1,0:T(8,128)(2,1)} %bitcast.14, bf16[4096,512]{0,1:T(8,128)(2,1)} %copy.10, f32[4096]{0:T(1024)S(1)} %add_rsqrt_fusion), kind=kOutput, calls=%fused_computation.30 | convolution fusion | flops 4301258752 | bytes 22036480 | tf_op jit(solution)/shard_map/dot_general | solution.py:34
  59.3 5.7 %copy-done = f32[1024,4096]{1,0:T(8,128)} copy-done((f32[1024,4096]{1,0:T(8,128)}, f32[1024,4096]{1,0:T(8,128)S(1)}, u32[]{:S(2)}) %copy-start) | copy-done | bytes 16777240
  65.0 1.5 fusion.18
  66.5 74.2 %psum.42 = f32[512]{0:T(512)S(1)} all-reduce(f32[512]{0:T(512)S(1)} %fusion.18), channel_id=1, replica_groups=mesh['dp'=8,'cls'=32] {'dp','cls'}, use_global_device_ids=true, to_apply=%region_4.0 | all-reduce | flops 512 | bytes 4096 | tf_op jit(solution)/shard_map/psum | solution.py:49
  140.8 4.4 divide_reduce_fusion
  145.2 10.2 %fusion.14 = (f32[512]{0:T(512)S(1)}, f32[512]{0:T(512)S(1)}, f32[512]{0:T(512)S(1)}, f32[512]{0:T(512)S(1)}) fusion(s32[4096]{0:T(1024)S(1)} %iota_add_fusion, s32[512]{0:T(512)S(1)} %get-tuple-element.12, f32[1024,4096]{1,0:T(8,128)} %copy-done, f32[4096]{0:T(1024)S(1)} %multiply_add_fusion, f32[512]{0:T(512)S(1)} %psum.42), kind=kLoop, calls=%fused_computation.19 | loop fusion | flops 31455232 | bytes 16822272 | tf_op jit(solution)/shard_map/reduce_sum | solution.py:47
  155.4 73.8 %all-reduce.3 = (f32[512]{0:T(512)S(1)}, f32[512]{0:T(512)S(1)}, f32[512]{0:T(512)S(1)}, f32[512]{0:T(512)S(1)}) all-reduce(f32[512]{0:T(512)S(1)} %get-tuple-element.10, f32[512]{0:T(512)S(1)} %get-tuple-element.11, f32[512]{0:T(512)S(1)} %get-tuple-element.9, f32[512]{0:T(512)S(1)} %get-tuple-element.8), channel_id=1, replica_groups=mesh['dp'=8,'cls'=32] {'dp','cls'}, use_global_device_ids=true, to_apply=%region_9.0 | all-reduce | flops 2048 | bytes 16384 | tf_op jit(solution)/shard_map/psum | solution.py:55
  229.2 9.6 %fusion.13 = bf16[512,4096]{1,0:T(8,128)(2,1)S(1)} fusion(f32[512]{0:T(512)S(1)} %get-tuple-element.14, f32[512]{0:T(512)S(1)} %get-tuple-element.15, s32[4096]{0:T(1024)S(1)} %iota_add_fusion, f32[512]{0:T(512)S(1)} %convert_element_type.34, s32[512]{0:T(512)S(1)} %get-tuple-element.12, f32[1024,4096]{1,0:T(8,128)} %copy-done, ...), kind=kLoop, calls=%fused_computation.18 | loop fusion | flops 35651584 | bytes 21014528 | tf_op jit(solution)/shard_map/convert_element_type | solution.py:79
  238.9 1.9 copy-done.3
  240.8 3.4 fusion.19
  244.2 6.4 %fusion.3 = (f32[4096]{0:T(1024)S(1)}, f32[4096,512]{0,1:T(8,128)S(1)}) fusion(bf16[4096,512]{0,1:T(8,128)(2,1)} %copy.10, f32[4096]{0:T(1024)S(1)} %add_rsqrt_fusion, bf16[512,4096]{1,0:T(8,128)(2,1)} %copy-done.3, bf16[2,512,512]{2,1,0:T(8,128)(2,1)S(1)} %copy-done.7), kind=kOutput, calls=%fused_computation.8 | convolution fusion | flops 2155868160 | bytes 17334272 | tf_op jit(solution)/shard_map/dot_general | solution.py:86
  250.7 3.5 fusion.6
  254.2 6.4 %copy.11 = bf16[4096,512]{1,0:T(8,128)(2,1)} copy(bf16[4096,512]{0,1:T(8,128)(2,1)} %fusion.6) | data formatting | bytes 8388608
  261.9 235.5 %all-reduce.6.cloned.1.call-done = f32[512,512]{1,0:T(8,128)} async-done(((f32[512,512]{1,0:T(8,128)}), f32[512,512]{1,0:T(8,128)}) %all-reduce.6.cloned.1.call-update) | async-done | bytes 1048592 | tf_op jit(solution)/shard_map/psum | solution.py:81
  497.4 1.1 fusion.29
  498.5 1.7 fusion.31
  (36 shorter events, 1.9 us)
Async XLA Ops:
  7.2 10.1 %copy-start.10 = (u32[256]{0:T(256)S(1)}, u32[256]{0:T(256)}, u32[]{:S(2)}) copy-start(u32[256]{0:T(256)} %constant.51) | copy-start | bytes 3076
  7.2 11.3 %copy-start.8 = (s32[64]{0:T(128)S(1)}, s32[64]{0:T(128)}, u32[]{:S(2)}) copy-start(s32[64]{0:T(128)} %param.11) | copy-start | bytes 772
  7.2 11.6 %copy-start.9 = (s32[64]{0:T(128)S(1)}, s32[64]{0:T(128)}, u32[]{:S(2)}) copy-start(s32[64]{0:T(128)} %param.10) | copy-start | bytes 772
  7.2 45.5 %all-gather.2.cloned.1.call-start = ((), (), s32[]{:S(2)}) async-start(), calls=%async_computation | async-start | bytes 1179648 | tf_op jit(solution)/shard_map/all_gather | solution.py:25
  10.9 486.5 %all-reduce.6.cloned.1.call-start = ((), (), s32[]{:S(2)}) async-start(), calls=%async_computation.1 | async-start | bytes 2097152 | tf_op jit(solution)/shard_map/psum | solution.py:81
  59.3 5.7 %copy-start = (f32[1024,4096]{1,0:T(8,128)}, f32[1024,4096]{1,0:T(8,128)S(1)}, u32[]{:S(2)}) copy-start(f32[1024,4096]{1,0:T(8,128)S(1)} %fusion.21) | copy-start | bytes 50331652
  65.0 80.1 %copy-start.6 = (f32[4096]{0:T(1024)S(1)}, f32[4096]{0:T(1024)}, u32[]{:S(2)}) copy-start(f32[4096]{0:T(1024)} %param.9) | copy-start | bytes 49156
  145.2 84.0 %copy-start.5 = (f32[4096]{0:T(1024)}, f32[4096]{0:T(1024)S(1)}, u32[]{:S(2)}) copy-start(f32[4096]{0:T(1024)S(1)} %multiply_add_fusion) | copy-start | bytes 49156
  229.2 11.6 %copy-start.1 = (bf16[4096,512]{0,1:T(8,128)(2,1)S(1)}, bf16[4096,512]{0,1:T(8,128)(2,1)}, u32[]{:S(2)}) copy-start(bf16[4096,512]{0,1:T(8,128)(2,1)} %copy.10) | copy-start | bytes 12582916
  238.9 1.9 copy-start.3
  240.8 3.4 copy-start.7
  244.2 6.5 %copy-start.2 = (bf16[4096,512]{0,1:T(8,128)(2,1)S(1)}, bf16[4096,512]{0,1:T(8,128)(2,1)}, u32[]{:S(2)}) copy-start(bf16[4096,512]{0,1:T(8,128)(2,1)} %copy.10) | copy-start | bytes 12582916
  254.2 243.2 %copy-start.4 = (bf16[64,512]{1,0:T(8,128)(2,1)S(1)}, bf16[64,512]{1,0:T(8,128)(2,1)}, u32[]{:S(2)}) copy-start(bf16[64,512]{1,0:T(8,128)(2,1)} %param.7) | copy-start | bytes 196612
Sparse Core Ops, SparseCore 0:
  11.0 41.6 all-gather.1
  244.3 252.9 all-reduce.5
where the time goes:
time: 509 us; the launch traced here: 508 us
  waiting for transfers between devices  250 us (49%)
  blocking collectives  164 us (32%)
  other arithmetic  39.3 us (8%)
  local copies, waits for them, and re-layouts  21.5 us (4%)
  between operations  16.7 us (3%)
  matrix products  16.4 us (3%)
    psum x1, waiting for transfers between devices, body(): unit_total = lax.psum(unit_part, ('dp', 'cls'))  235 us
    psum x1, blocking collectives, body(): teacher_total = lax.psum(teach_part, ('dp', 'cls'))  74.2 us
    psum x1, blocking collectives, body(): aligned_total, aligned_cross = lax.psum((q_part, r_part), ('dp', 'cls'))  73.8 us
    unnamed x29, local copies, waits for them, and re-layouts  21.5 us
    unnamed x1, blocking collectives  16.2 us
    all_gather x1, waiting for transfers between devices, body(): lax.all_gather(stacked, 'dp', axis=1, tiled=True)  14.4 us
    reduce_sum x1, other arithmetic, body(): label_part = jnp.sum(hit * stud, axis=1)  10.2 us
  transfers between devices with their start and end apart: 2, of which 2 were waited for; matrix products, arithmetic and copies ran while one was open for 5% of the time, Pallas kernels for 0%

commit v1 on v0

--- a/solution.py
+++ b/solution.py
@@ -46,7 +46,8 @@
     stud_part = jnp.sum(jnp.exp(stud - SCALE), axis=1)
     label_part = jnp.sum(hit * stud, axis=1)
     classes_total = cls_dev * lax.axis_size("dp") * lax.axis_size("cls")
-    teacher_total = lax.psum(teach_part, ("dp", "cls"))
+    parts = lax.all_gather(teach_part, ("dp", "cls"))
+    teacher_total = jnp.sum(parts, axis=0)
     share = teach / teacher_total[:, None]
     batch = classes_total / row_count * jnp.sum(share, axis=0)
     fresh = MOMENTUM * marginal + (1.0 - MOMENTUM) * batch

time: 509 us -> 503 us (0.988)
  blocking collectives: 164 us -> 158 us
    psum x1 -> x0, blocking collectives: 74.2 us -> none  [body(): teacher_total = lax.psum(teach_part, ('dp', 'cls'))]
    all_gather x0 -> x1, blocking collectives: none -> 66.6 us  [body(): parts = lax.all_gather(teach_part, ('dp', 'cls'))]
where the time goes in v1:
time: 503 us; the launch traced here: 502 us
  waiting for transfers between devices  250 us (50%)
  blocking collectives  158 us (31%)
  other arithmetic  39.6 us (8%)
  local copies, waits for them, and re-layouts  21.5 us (4%)
  between operations  16.7 us (3%)
  matrix products  16.4 us (3%)
    psum x1, waiting for transfers between devices, body(): unit_total = lax.psum(unit_part, ('dp', 'cls'))  236 us
    psum x1, blocking collectives, body(): aligned_total, aligned_cross = lax.psum((q_part, r_part), ('dp', 'cls'))  74.8 us
    all_gather x1, blocking collectives, body(): parts = lax.all_gather(teach_part, ('dp', 'cls'))  66.6 us
    unnamed x29, local copies, waits for them, and re-layouts  21.5 us
    unnamed x1, blocking collectives  16.2 us
    all_gather x1, waiting for transfers between devices, body(): lax.all_gather(stacked, 'dp', axis=1, tiled=True)  14.4 us
    reduce_sum x1, other arithmetic, body(): label_part = jnp.sum(hit * stud, axis=1)  10.2 us
  transfers between devices with their start and end apart: 2, of which 2 were waited for; matrix products, arithmetic and copies ran while one was open for 5% of the time, Pallas kernels for 0%

profile of v1, /device:TPU:2, one launch (start us, length us, event | category | flops | bytes accessed | tf_op | source)
XLA Modules:
  0.0 502.0 jit_solution(6218699096904499758)
XLA Ops:
  7.2 1.0 fusion.32
  8.2 1.0 fusion.27
  9.2 1.0 fusion.33
  10.2 0.7 pad_maximum_fusion
  10.9 6.3 %copy.12 = bf16[4096,512]{0,1:T(8,128)(2,1)} copy(bf16[4096,512]{1,0:T(8,128)(2,1)} %param.8) | data formatting | bytes 8388608 | tf_op args[2]
  19.0 16.2 %all-reduce.2 = (s32[512]{0:T(512)S(1)}, s32[512]{0:T(512)S(1)}) all-reduce(s32[512]{0:T(512)S(1)} %dynamic-update-slice.1, s32[512]{0:T(512)S(1)} %dynamic-update-slice), channel_id=1, replica_groups=mesh['dp'=8,'cls'=32] {'dp'}, use_global_device_ids=true, to_apply=%add.1 | all-reduce | flops 1024 | bytes 8192
  35.2 3.1 fusion.7
  38.3 14.4 %all-gather.4.cloned.1.call-done = bf16[2,512,512]{2,1,0:T(8,128)(2,1)} async-done(((bf16[2,64,512]{2,1,0:T(8,128)(2,1)}), bf16[2,512,512]{2,1,0:T(8,128)(2,1)}) %all-gather.4.cloned.1.call-update) | async-done | bytes 1048592 | tf_op jit(solution)/shard_map/all_gather | solution.py:25
  52.7 6.6 %fusion.21 = f32[1024,4096]{1,0:T(8,128)S(1)} fusion(bf16[1024,512]{1,0:T(8,128)(2,1)} %bitcast.16, bf16[4096,512]{0,1:T(8,128)(2,1)} %copy.12, f32[4096]{0:T(1024)S(1)} %add_rsqrt_fusion), kind=kOutput, calls=%fused_computation.30 | convolution fusion | flops 4301258752 | bytes 22036480 | tf_op jit(solution)/shard_map/dot_general | solution.py:34
  59.3 5.7 %copy-done = f32[1024,4096]{1,0:T(8,128)} copy-done((f32[1024,4096]{1,0:T(8,128)}, f32[1024,4096]{1,0:T(8,128)S(1)}, u32[]{:S(2)}) %copy-start) | copy-done | bytes 16777240
  65.0 1.5 fusion.18
  66.5 66.6 %all-gather.1 = f32[256,1,512]{2,1,0:T(1,128)S(1)} all-gather(f32[1,1,512]{2,1,0:T(1,128)S(1)} %bitcast.15), channel_id=2, replica_groups=mesh['dp'=8,'cls'=32] {'dp','cls'}, dimensions={0}, use_global_device_ids=true | all-gather | bytes 526336 | tf_op jit(solution)/shard_map/all_gather | solution.py:49
  133.5 4.4 divide_reduce_fusion
  138.0 10.2 %fusion.14 = (f32[512]{0:T(512)S(1)}, f32[512]{0:T(512)S(1)}, f32[512]{0:T(512)S(1)}, f32[512]{0:T(512)S(1)}) fusion(s32[4096]{0:T(1024)S(1)} %iota_add_fusion, s32[512]{0:T(512)S(1)} %get-tuple-element.16, f32[1024,4096]{1,0:T(8,128)} %copy-done, f32[4096]{0:T(1024)S(1)} %multiply_add_fusion, f32[512]{0:T(512)S(1)} %reduce_sum.121), kind=kLoop, calls=%fused_computation.19 | loop fusion | flops 31455232 | bytes 16822272 | tf_op jit(solution)/shard_map/reduce_sum | solution.py:47
  148.2 74.8 %all-reduce.3 = (f32[512]{0:T(512)S(1)}, f32[512]{0:T(512)S(1)}, f32[512]{0:T(512)S(1)}, f32[512]{0:T(512)S(1)}) all-reduce(f32[512]{0:T(512)S(1)} %get-tuple-element.14, f32[512]{0:T(512)S(1)} %get-tuple-element.15, f32[512]{0:T(512)S(1)} %get-tuple-element.13, ...), channel_id=1, replica_groups=mesh['dp'=8,'cls'=32] {'dp','cls'}, use_global_device_ids=true, to_apply=%region_9.0 | all-reduce | flops 2048 | bytes 16384 | tf_op jit(solution)/shard_map/psum | solution.py:56
  223.0 9.6 %fusion.13 = bf16[512,4096]{1,0:T(8,128)(2,1)S(1)} fusion(f32[512]{0:T(512)S(1)} %get-tuple-element.18, f32[512]{0:T(512)S(1)} %get-tuple-element.19, s32[4096]{0:T(1024)S(1)} %iota_add_fusion, f32[512]{0:T(512)S(1)} %convert_element_type.34, s32[512]{0:T(512)S(1)} %get-tuple-element.16, f32[1024,4096]{1,0:T(8,128)} %copy-done, ...), kind=kLoop, calls=%fused_computation.18 | loop fusion | flops 35651584 | bytes 21014528 | tf_op jit(solution)/shard_map/convert_element_type | solution.py:80
  232.6 1.9 copy-done.3
  234.6 3.4 fusion.19
  238.0 6.4 %fusion.3 = (f32[4096]{0:T(1024)S(1)}, f32[4096,512]{0,1:T(8,128)S(1)}) fusion(bf16[4096,512]{0,1:T(8,128)(2,1)} %copy.12, f32[4096]{0:T(1024)S(1)} %add_rsqrt_fusion, bf16[512,4096]{1,0:T(8,128)(2,1)} %copy-done.3, bf16[2,512,512]{2,1,0:T(8,128)(2,1)S(1)} %copy-done.7), kind=kOutput, calls=%fused_computation.8 | convolution fusion | flops 2155868160 | bytes 17334272 | tf_op jit(solution)/shard_map/dot_general | solution.py:87
  244.5 3.5 fusion.6
  248.0 6.4 %copy.13 = bf16[4096,512]{1,0:T(8,128)(2,1)} copy(bf16[4096,512]{0,1:T(8,128)(2,1)} %fusion.6) | data formatting | bytes 8388608
  255.7 235.6 %all-reduce.6.cloned.1.call-done = f32[512,512]{1,0:T(8,128)} async-done(((f32[512,512]{1,0:T(8,128)}), f32[512,512]{1,0:T(8,128)}) %all-reduce.6.cloned.1.call-update) | async-done | bytes 1048592 | tf_op jit(solution)/shard_map/psum | solution.py:82
  491.3 1.1 fusion.29
  492.4 1.7 fusion.31
  (37 shorter events, 2.2 us)
Async XLA Ops:
  7.2 10.1 %copy-start.10 = (u32[256]{0:T(256)S(1)}, u32[256]{0:T(256)}, u32[]{:S(2)}) copy-start(u32[256]{0:T(256)} %constant.51) | copy-start | bytes 3076
  7.2 11.3 %copy-start.8 = (s32[64]{0:T(128)S(1)}, s32[64]{0:T(128)}, u32[]{:S(2)}) copy-start(s32[64]{0:T(128)} %param.11) | copy-start | bytes 772
  7.2 11.6 %copy-start.9 = (s32[64]{0:T(128)S(1)}, s32[64]{0:T(128)}, u32[]{:S(2)}) copy-start(s32[64]{0:T(128)} %param.10) | copy-start | bytes 772
  7.2 45.5 %all-gather.4.cloned.1.call-start = ((), (), s32[]{:S(2)}) async-start(), calls=%async_computation | async-start | bytes 1179648 | tf_op jit(solution)/shard_map/all_gather | solution.py:25
  10.9 480.4 %all-reduce.6.cloned.1.call-start = ((), (), s32[]{:S(2)}) async-start(), calls=%async_computation.1 | async-start | bytes 2097152 | tf_op jit(solution)/shard_map/psum | solution.py:82
  59.3 5.7 %copy-start = (f32[1024,4096]{1,0:T(8,128)}, f32[1024,4096]{1,0:T(8,128)S(1)}, u32[]{:S(2)}) copy-start(f32[1024,4096]{1,0:T(8,128)S(1)} %fusion.21) | copy-start | bytes 50331652
  65.0 72.9 %copy-start.6 = (f32[4096]{0:T(1024)S(1)}, f32[4096]{0:T(1024)}, u32[]{:S(2)}) copy-start(f32[4096]{0:T(1024)} %param.9) | copy-start | bytes 49156
  137.9 85.1 %copy-start.5 = (f32[4096]{0:T(1024)}, f32[4096]{0:T(1024)S(1)}, u32[]{:S(2)}) copy-start(f32[4096]{0:T(1024)S(1)} %multiply_add_fusion) | copy-start | bytes 49156
  223.0 11.6 %copy-start.1 = (bf16[4096,512]{0,1:T(8,128)(2,1)S(1)}, bf16[4096,512]{0,1:T(8,128)(2,1)}, u32[]{:S(2)}) copy-start(bf16[4096,512]{0,1:T(8,128)(2,1)} %copy.12) | copy-start | bytes 12582916
  232.6 1.9 copy-start.3
  234.6 3.4 copy-start.7
  238.0 6.5 %copy-start.2 = (bf16[4096,512]{0,1:T(8,128)(2,1)S(1)}, bf16[4096,512]{0,1:T(8,128)(2,1)}, u32[]{:S(2)}) copy-start(bf16[4096,512]{0,1:T(8,128)(2,1)} %copy.12) | copy-start | bytes 12582916
  248.0 243.3 %copy-start.4 = (bf16[64,512]{1,0:T(8,128)(2,1)S(1)}, bf16[64,512]{1,0:T(8,128)(2,1)}, u32[]{:S(2)}) copy-start(bf16[64,512]{1,0:T(8,128)(2,1)} %param.7) | copy-start | bytes 196612
Sparse Core Ops, SparseCore 0:
  11.0 41.6 all-gather.3
  238.1 253.1 all-reduce.5
